TPU v7x, 32 devices: a whole 2x2x4 slice. The times are simulated.
32 devices in a mesh: dom: 16 (over z, y, x), band: 2 (over core).
Axes of the slice: x: 2, y: 2, z: 4, core: 2. Of those that a mesh axis runs over, the one named last changes fastest.
Arguments:
- wave: float32 [8, 64, 64, 128], P('band', 'dom'), parts along dimension 0, may hold values from -6 to 6
- potential: float32 [64, 64, 128], P('dom'), may hold values from -6 to 6
- energies: float32 [8], P('band'), parts along dimension 0, may hold values from -1 to 1
- proj_index: int32 [512, 256], P('dom'), may hold values from 0 to 32767
- proj_values: float32 [512, 8, 256], P('dom'), may hold values from -4 to 4
- slot_atom: int32 [512], P('dom'), may hold values from 0 to 384, as said below
- atom_rank: int32 [384], replicated, may hold values from 0 to 383, as said below
- d_matrix: float32 [384, 8, 8], P('dom'), may hold values from -5 to 5
- q_matrix: float32 [384, 8, 8], P('dom'), may hold values from -5 to 5
Outputs:
- residual: float32 [8, 64, 64, 128], P('band', 'dom'), parts along dimension 0
There are 2 independent parts, one for each index of `band`. A program takes and returns all parts, laid end to end along the dimension named above; an argument that names none is the same for every part. Nothing has to cross between parts.
Inputs may be any that keep to these rules, and one draw needn't show every extreme that they name: `slot_atom`: every device holds at least 8 live slots, live slots come first among a device's slots, and in every draw some device has all 32 slots live and some has only 8. The atom of a live slot on device d has atom_rank // 24 within 2 of d, counted cyclically over the devices. `atom_rank`: A permutation of the atoms.
All inputs are finite; a program needn't handle non-finite values.
Results may differ from a plain program's by a relative error of at most 0.00007.
Values sent between devices are 32-bit elements; how exact they have to be, the bound alone decides.
A program may use at most 64 MiB of HBM per device.

v0:
```python
import jax
import jax.numpy as jnp
from jax import lax
from jax.sharding import PartitionSpec as P

HIGH = lax.Precision.HIGHEST


def extended(block, sides, width):
    for axis, dim in sides:
        count = lax.axis_size(axis)
        forward = [(i, i + 1) for i in range(count - 1)]
        forward.append((count - 1, 0))
        backward = [(target, source) for source, target in forward]
        low = lax.ppermute(
            lax.slice_in_dim(block, block.shape[dim] - width, None, axis=dim), axis, forward
        )
        high = lax.ppermute(lax.slice_in_dim(block, 0, width, axis=dim), axis, backward)
        block = jnp.concatenate([low, block, high], axis=dim)
    return block


def shifted(value, axis, steps):
    count = lax.axis_size(axis)
    pairs = [(source, (source + steps) % count) for source in range(count)]
    return lax.ppermute(value, axis, pairs)


def inner_axes(field, operator):
    total = operator
    for axis in (2, 3):
        total = total - 2.5 * field
        total = total + 4.0 / 3.0 * (jnp.roll(field, 1, axis) + jnp.roll(field, -1, axis))
        total = total - 1.0 / 12.0 * (jnp.roll(field, 2, axis) + jnp.roll(field, -2, axis))
    return total


def weigh(rows, d_part, q_part, energies, bands, nproj):
    coeffs = rows.reshape(rows.shape[0], bands, nproj)
    weight = jnp.einsum("aij,anj->ani", d_part, coeffs, precision=HIGH)
    weight = weight - energies[None, :, None] * jnp.einsum(
        "aij,anj->ani", q_part, coeffs, precision=HIGH
    )
    return weight.reshape(rows.shape[0], bands * nproj)


def per_device(
    wave, potential, energies, proj_index, proj_values, slot_atom, atom_rank, d_matrix, q_matrix
):
    bands = wave.shape[0]
    slot_count = proj_index.shape[0]
    nproj = proj_values.shape[1]
    atoms_all = atom_rank.shape[0]
    atoms_dev = d_matrix.shape[0]
    n_dom = lax.axis_size("dom")
    padded = extended(wave, (("dom", 1),), 2)
    center = padded[:, 2:-2]
    along_x = (
        -2.5 * center
        + 4.0 / 3.0 * (padded[:, 3:-1] + padded[:, 1:-3])
        - 1.0 / 12.0 * (padded[:, 4:] + padded[:, :-4])
    )
    laplace_all = inner_axes(center, along_x)
    local = -0.5 * laplace_all + (potential[None] - energies[:, None, None, None]) * center
    flat_index = proj_index.reshape(-1)
    picked = jnp.take(center.reshape(bands, -1), flat_index, axis=1).reshape(bands, slot_count, -1)
    coeff = jnp.einsum("nsp,sip->sni", picked, proj_values, precision=HIGH).reshape(
        slot_count, bands * nproj
    )
    live = slot_atom < atoms_all
    position = jnp.where(live, atom_rank[jnp.minimum(slot_atom, atoms_all - 1)], 0)
    myself = lax.axis_index("dom")
    offset = (position // atoms_dev - myself + 2 + n_dom) % n_dom
    column = jnp.where(live, offset * atoms_dev + position % atoms_dev, 5 * atoms_dev)
    table = (column[:, None] == jnp.arange(5 * atoms_dev, dtype=jnp.int32)[None, :]).astype(
        jnp.float32
    )
    partial_value = jnp.einsum("sa,sk->ak", table, coeff, precision=HIGH)

    def block(step):
        return partial_value[(step + 2) * atoms_dev : (step + 3) * atoms_dev]

    total = block(0)
    for step in (-2, -1, 1, 2):
        total = total + shifted(block(step), "dom", step)
    weighted = weigh(total, d_matrix, q_matrix, energies, bands, nproj)
    windows = {0: weighted}
    for step in (-2, -1, 1, 2):
        windows[step] = shifted(weighted, "dom", -step)
    stacked = jnp.concatenate(
        [windows[-2], windows[-1], windows[0], windows[1], windows[2]], axis=0
    )
    slot_weight = jnp.dot(table, stacked, precision=HIGH).reshape(slot_count, bands, nproj)
    back = jnp.einsum("sni,sip->nsp", slot_weight, proj_values, precision=HIGH).reshape(bands, -1)
    result = local.reshape(bands, -1).at[:, flat_index].add(back)
    return result.reshape(wave.shape)


def solution(mesh):
    placed = (
        P("band", "dom", None, None),
        P("dom", None, None),
        P("band"),
        P("dom", None),
        P("dom", None, None),
        P("dom"),
        P(),
        P("dom", None, None),
        P("dom", None, None),
    )
    return jax.shard_map(
        per_device,
        mesh=mesh,
        in_specs=placed,
        out_specs=P("band", "dom", None, None),
        check_vma=False,
    )
```

profile of v0, /device:TPU:0, one launch (start us, length us, event | category | flops | bytes accessed | tf_op | source)
XLA Modules:
  0.0 157.0 jit_solution(15287305900644604843)
XLA Ops:
  0.0 0.8 compare_and_fusion
  1.7 9.7 %copy.19 = f32[4,4,64,128]{0,3,2,1:T(8,128)} copy(f32[4,4,64,128]{3,2,1,0:T(8,128)} %param.9) | data formatting | bytes 1048576 | tf_op args[0]
  11.5 33.5 %gather_fusion.1 = f32[8192,4]{1,0:T(8,128)} fusion(f32[4,32768]{0,1:T(8,128)} %bitcast.34, s32[8192]{0:T(1024)S(1)} %broadcast_clamp_fusion), kind=kCustom, calls=%fused_computation.1 | custom fusion | bytes 294912 | tf_op jit(solution)/shard_map/jit(_take)/gather | solution.py:66
  45.0 2.8 %copy.20 = f32[4,32,256]{2,0,1:T(4,128)S(1)} copy(f32[4,32,256]{0,2,1:T(8,128)} %bitcast.35) | data formatting | bytes 262144 | tf_op jit(solution)/shard_map/jit(_take)/gather | solution.py:66
  50.0 6.0 %collective-permute-start.2 = (f32[24,32]{0,1:T(8,128)}, f32[24,32]{0,1:T(8,128)S(1)}, u32[]{:S(2)}, u32[]{:S(2)}) collective-permute-start(f32[24,32]{0,1:T(8,128)} %get-tuple-element.25), channel_id=1, source_target_pairs={{0,28},{2,30},{4,0},{6,2},{8,4},{10,6},{12,8},{14,10},{16,12},{18,... | collective-permute-start | bytes 9224 | tf_op jit(solution)/shard_map/ppermute | solution.py:26
  56.0 1.4 collective-permute-start.3
  58.0 0.9 collective-permute-start.5
  58.9 0.8 fusion.40
  59.8 1.5 collective-permute-start.1
  61.7 1.1 fusion.36
  62.7 1.0 fusion.38
  63.8 1.1 fusion.32
  64.9 1.1 fusion.33
  66.5 1.0 convolution_multiply_fusion
  68.6 4.9 %collective-permute-start.8 = (f32[24,32]{0,1:T(8,128)S(1)}, f32[24,32]{0,1:T(8,128)S(1)}, u32[]{:S(2)}, u32[]{:S(2)}) collective-permute-start(f32[24,32]{0,1:T(8,128)S(1)} %bitcast.43), channel_id=1, source_target_pairs={{0,30},{2,0},{4,2},{6,4},{8,6},{10,8},{12,10},{14,12},{16,14},{18,... | collective-permute-start | bytes 9224 | tf_op jit(solution)/shard_map/ppermute | solution.py:26
  73.5 2.0 %collective-permute-start.9 = (f32[24,32]{0,1:T(8,128)S(1)}, f32[24,32]{0,1:T(8,128)S(1)}, u32[]{:S(2)}, u32[]{:S(2)}) collective-permute-start(f32[24,32]{0,1:T(8,128)S(1)} %bitcast.44), channel_id=1, source_target_pairs={{0,28},{2,30},{4,0},{6,2},{8,4},{10,6},{12,8},{14,10},{16,12},{18,... | collective-permute-start | bytes 9224 | tf_op jit(solution)/shard_map/ppermute | solution.py:26
  76.1 1.1 collective-permute-done.9
  78.6 2.6 %copy.29 = f32[8192,4]{1,0:T(8,128)} copy(f32[8192,4]{0,1:T(4,128)S(1)} %bitcast.36) | data formatting | bytes 262144 | tf_op jit(solution)/shard_map/reshape | solution.py:94
  81.3 0.9 collective-permute-done
  82.3 1.0 constant_dynamic-update-slice_fusion
  83.3 3.1 %fusion.9 = f32[4,4,64,128]{3,2,1,0:T(8,128)S(1)} fusion(f32[4,6,64,128]{3,2,1,0:T(8,128)S(1)} %get-tuple-element.24, f32[4,6,64,128]{3,2,1,0:T(8,128)S(1)} %constant_dynamic-update-slice_fusion, f32[4,4,63,128]{3,2,1,0:T(8,128)} %get-tuple-element.18, f32[4,4,1,128]{3,2,1,0:T(1,128)S(1)} %get-tuple-element.20, f32[4,4,1,128]{3,2,1,0:T(1,128)S(1)} %get-tuple-element.19, ...), kind=kLoop, calls=%fused_computation.16 | loop fusion | flops 4456448 | bytes 7471120 | tf_op jit(solution)/shard_map/add | solution.py:64
  86.3 8.7 %copy.18 = f32[4,4,64,128]{0,3,2,1:T(8,128)} copy(f32[4,4,64,128]{3,2,1,0:T(8,128)S(1)} %fusion.9) | data formatting | bytes 1048576 | tf_op jit(solution)/shard_map/add | solution.py:64
  95.0 51.3 %scatter_fusion = f32[4,32768]{0,1:T(8,128)} fusion(f32[4,32768]{0,1:T(8,128)} %bitcast.32, s32[8192]{0:T(1024)S(1)} %bitcast.38, f32[8192,4]{1,0:T(8,128)} %copy.29), kind=kCustom, calls=%fused_computation.2 | custom fusion | flops 32768 | bytes 425984 | tf_op jit(solution)/shard_map/scatter-add | solution.py:95
  146.3 10.7 %copy.30 = f32[4,4,64,128]{3,2,1,0:T(8,128)} copy(f32[4,4,64,128]{0,3,2,1:T(8,128)} %bitcast.33) | data formatting | bytes 1048576 | tf_op jit(solution)/shard_map/reshape | solution.py:96
  (53 shorter events, 7.5 us)
Async XLA Ops:
  0.0 47.8 %copy-start = (f32[32,8,256]{2,1,0:T(8,128)S(1)}, f32[32,8,256]{2,1,0:T(8,128)}, u32[]{:S(2)}) copy-start(f32[32,8,256]{2,1,0:T(8,128)} %param.13) | copy-start | bytes 786436
  0.0 58.9 %copy-start.1 = (f32[4,4,64,128]{3,2,1,0:T(8,128)S(1)}, f32[4,4,64,128]{3,2,1,0:T(8,128)}, u32[]{:S(2)}) copy-start(f32[4,4,64,128]{3,2,1,0:T(8,128)} %param.9) | copy-start | bytes 1572868
  0.0 48.3 %copy-start.5 = (s32[32]{0:T(128)S(1)}, s32[32]{0:T(128)}, u32[]{:S(2)}) copy-start(s32[32]{0:T(128)} %param.14) | copy-start | bytes 388
  0.0 48.3 %copy-start.2 = (s32[384]{0:T(512)S(1)}, s32[384]{0:T(512)}, u32[]{:S(2)}) copy-start(s32[384]{0:T(512)} %param.15) | copy-start | bytes 4612
  1.7 64.3 %copy-start.3 = (f32[24,8,8]{0,2,1:T(8,128)S(1)}, f32[24,8,8]{0,2,1:T(8,128)}, u32[]{:S(2)}) copy-start(f32[24,8,8]{0,2,1:T(8,128)} %param.17) | copy-start | bytes 18436
  1.7 64.4 %copy-start.4 = (f32[24,8,8]{0,2,1:T(8,128)S(1)}, f32[24,8,8]{0,2,1:T(8,128)}, u32[]{:S(2)}) copy-start(f32[24,8,8]{0,2,1:T(8,128)} %param.16) | copy-start | bytes 18436
  49.1 15.8 %copy-start.6 = (s32[32]{0:T(128)}, s32[32]{0:T(128)S(1)}, u32[]{:S(2)}) copy-start(s32[32]{0:T(128)S(1)} %compare_select_fusion.5) | copy-start | bytes 388
  50.0 16.3 %collective-permute-start.2 = (f32[24,32]{0,1:T(8,128)}, f32[24,32]{0,1:T(8,128)S(1)}, u32[]{:S(2)}, u32[]{:S(2)}) collective-permute-start(f32[24,32]{0,1:T(8,128)} %get-tuple-element.25), channel_id=1, source_target_pairs={{0,28},{2,30},{4,0},{6,2},{8,4},{10,6},{12,8},{14,10},{16,12},{18,... | collective-permute-start | bytes 9224 | tf_op jit(solution)/shard_map/ppermute | solution.py:26
  56.0 10.3 %collective-permute-start.3 = (f32[24,32]{0,1:T(8,128)}, f32[24,32]{0,1:T(8,128)S(1)}, u32[]{:S(2)}, u32[]{:S(2)}) collective-permute-start(f32[24,32]{0,1:T(8,128)} %get-tuple-element.28), channel_id=1, source_target_pairs={{0,30},{2,0},{4,2},{6,4},{8,6},{10,8},{12,10},{14,12},{16,14},{18,... | collective-permute-start | bytes 9224 | tf_op jit(solution)/shard_map/ppermute | solution.py:26
  57.4 8.9 %collective-permute-start.4 = (f32[24,32]{0,1:T(8,128)S(1)}, f32[24,32]{0,1:T(8,128)S(1)}, u32[]{:S(2)}, u32[]{:S(2)}) collective-permute-start(f32[24,32]{0,1:T(8,128)S(1)} %get-tuple-element.27), channel_id=1, source_target_pairs={{0,2},{2,4},{4,6},{6,8},{8,10},{10,12},{12,14},{14,16},{16,18},{18... | collective-permute-start | bytes 9224 | tf_op jit(solution)/shard_map/ppermute | solution.py:26
  58.0 8.3 %collective-permute-start.5 = (f32[24,32]{0,1:T(8,128)S(1)}, f32[24,32]{0,1:T(8,128)S(1)}, u32[]{:S(2)}, u32[]{:S(2)}) collective-permute-start(f32[24,32]{0,1:T(8,128)S(1)} %get-tuple-element.26), channel_id=1, source_target_pairs={{0,4},{2,6},{4,8},{6,10},{8,12},{10,14},{12,16},{14,18},{16,20},{1... | collective-permute-start | bytes 9224 | tf_op jit(solution)/shard_map/ppermute | solution.py:26
  59.8 21.4 %collective-permute-start.1 = (f32[4,2,64,128]{3,2,1,0:T(8,128)}, f32[4,2,64,128]{3,2,1,0:T(8,128)S(1)}, u32[]{:S(2)}, u32[]{:S(2)}) collective-permute-start(f32[4,2,64,128]{3,2,1,0:T(8,128)} %get-tuple-element.22), channel_id=1, source_target_pairs={{0,2},{2,4},{4,6},{6,8},{8,10},{10,12},{12,14},{14,16},{16,18},{18... | collective-permute-start | bytes 786440 | tf_op jit(solution)/shard_map/ppermute | solution.py:15
  67.8 7.7 %collective-permute-start.6 = (f32[24,32]{0,1:T(8,128)S(1)}, f32[24,32]{0,1:T(8,128)S(1)}, u32[]{:S(2)}, u32[]{:S(2)}) collective-permute-start(f32[24,32]{0,1:T(8,128)S(1)} %bitcast.41), channel_id=1, source_target_pairs={{0,4},{2,6},{4,8},{6,10},{8,12},{10,14},{12,16},{14,18},{16,20},{1... | collective-permute-start | bytes 9224 | tf_op jit(solution)/shard_map/ppermute | solution.py:26
  67.8 8.3 %collective-permute-start.7 = (f32[24,32]{0,1:T(8,128)S(1)}, f32[24,32]{0,1:T(8,128)S(1)}, u32[]{:S(2)}, u32[]{:S(2)}) collective-permute-start(f32[24,32]{0,1:T(8,128)S(1)} %bitcast.42), channel_id=1, source_target_pairs={{0,2},{2,4},{4,6},{6,8},{8,10},{10,12},{12,14},{14,16},{16,18},{18... | collective-permute-start | bytes 9224 | tf_op jit(solution)/shard_map/ppermute | solution.py:26
  68.6 7.5 %collective-permute-start.8 = (f32[24,32]{0,1:T(8,128)S(1)}, f32[24,32]{0,1:T(8,128)S(1)}, u32[]{:S(2)}, u32[]{:S(2)}) collective-permute-start(f32[24,32]{0,1:T(8,128)S(1)} %bitcast.43), channel_id=1, source_target_pairs={{0,30},{2,0},{4,2},{6,4},{8,6},{10,8},{12,10},{14,12},{16,14},{18,... | collective-permute-start | bytes 9224 | tf_op jit(solution)/shard_map/ppermute | solution.py:26
  73.5 3.7 %collective-permute-start.9 = (f32[24,32]{0,1:T(8,128)S(1)}, f32[24,32]{0,1:T(8,128)S(1)}, u32[]{:S(2)}, u32[]{:S(2)}) collective-permute-start(f32[24,32]{0,1:T(8,128)S(1)} %bitcast.44), channel_id=1, source_target_pairs={{0,28},{2,30},{4,0},{6,2},{8,4},{10,6},{12,8},{14,10},{16,12},{18,... | collective-permute-start | bytes 9224 | tf_op jit(solution)/shard_map/ppermute | solution.py:26
  75.5 6.7 %collective-permute-start = (f32[4,2,64,128]{3,2,1,0:T(8,128)}, f32[4,2,64,128]{3,2,1,0:T(8,128)}, u32[]{:S(2)}, u32[]{:S(2)}) collective-permute-start(f32[4,2,64,128]{3,2,1,0:T(8,128)} %get-tuple-element.21), channel_id=1, source_target_pairs={{2,0},{4,2},{6,4},{8,6},{10,8},{12,10},{14,12},{16,14},{18,16},{20... | collective-permute-start | bytes 786440 | tf_op jit(solution)/shard_map/ppermute | solution.py:18
where the time goes:
time: 158 us; the launch traced here: 157 us
  local copies, waits for them, and re-layouts  77.6 us (49%)
  other arithmetic  55.4 us (35%)
  starting transfers between devices  18.7 us (12%)
  matrix products  2.96 us (2%)
  waiting for transfers between devices  2.08 us (1%)
    scatter-add x1, other arithmetic, per_device(): result = local.reshape(bands, -1).at[:, flat_index].add(back)  51.3 us
    gather x2, local copies, waits for them, and re-layouts, per_device(): jnp.take(center.reshape(bands, -1), flat_index, axis=1)  36.3 us
    ppermute x8, starting transfers between devices, shifted(): return lax.ppermute(value, axis, pairs)  16.7 us
    unnamed x20, local copies, waits for them, and re-layouts  10.9 us
    reshape x1, local copies, waits for them, and re-layouts, per_device(): return result.reshape(wave.shape)  10.7 us
    add x1, local copies, waits for them, and re-layouts, per_device(): -0.5 * laplace_all  8.67 us
    slice x4, local copies, waits for them, and re-layouts, inner_axes(): jnp.roll(field, -2, axis)  3.33 us
  transfers between devices with their start and end apart: 10, of which 2 were waited for; matrix products, arithmetic and copies ran while one was open for 7% of the time, Pallas kernels for 0%

commit v1 on v0

v1 whole, which is shorter than its diff:
```python
import functools

import jax
import jax.numpy as jnp
from jax import lax
from jax.experimental import pallas as pl
from jax.experimental.pallas import tpu as pltpu
from jax.sharding import PartitionSpec as P

HIGH = lax.Precision.HIGHEST
MESH = pl.DeviceIdType.MESH
STEPS = (-2, -1, 1, 2)
LANES = 128


def log2(size):
    bits = size.bit_length() - 1
    assert size == 1 << bits
    return bits


def iota(shape, dim):
    return lax.broadcasted_iota(jnp.int32, shape, dim)


def ones_where(mask):
    return jnp.where(mask, 1.0, 0.0).astype(jnp.float32)


def dot(a, b):
    return jnp.dot(a, b, precision=HIGH, preferred_element_type=jnp.float32)


def dot_dims(a, b, left, right, precision=None):
    return lax.dot_general(
        a, b, (((left,), (right,)), ((), ())),
        precision=precision, preferred_element_type=jnp.float32,
    )


def halves(value):
    high = value.astype(jnp.bfloat16)
    low = (value - high.astype(jnp.float32)).astype(jnp.bfloat16)
    return high, low


def kernel(
    n_dom, unroll,
    energies, wave, potential, index, values, slot_atom, atom_rank, effective,
    out,
    low_halo, high_halo, turned, row_hot, col_hot, picked, back_rows, acc,
    parts, arrived, windows, send_sem, recv_sem,
):
    bands, planes, ny, nz = wave.shape
    slots, pts = index.shape
    nproj = values.shape[0] // slots
    atoms_dev = effective.shape[0]
    atoms_all = atom_rank.shape[1]
    rows = planes * ny
    wide = bands * nz
    row_shift, lane_mask = log2(nz), nz - 1
    p_bits, s_bits = log2(nproj), log2(slots)

    me = lax.axis_index("dom")

    def device(step):
        return lax.rem(me + step + n_dom, n_dom)

    barrier = pltpu.get_barrier_semaphore()
    for step in STEPS:
        pl.semaphore_signal(barrier, inc=1, device_id={"dom": device(step)}, device_id_type=MESH)

    for n in range(bands):
        block = wave[n].reshape(rows, nz).T
        high, low = halves(block)
        turned[n * nz : (n + 1) * nz, :rows] = high
        turned[n * nz : (n + 1) * nz, rows:] = low

    pl.semaphore_wait(barrier, len(STEPS))

    def copy(k, src, dst, step):
        return pltpu.make_async_remote_copy(
            src_ref=src, dst_ref=dst, send_sem=send_sem.at[k], recv_sem=recv_sem.at[k],
            device_id={"dom": device(step)}, device_id_type=MESH,
        )

    halo = [
        copy(0, wave.at[:, planes - 2 : planes], low_halo, 1),
        copy(1, wave.at[:, 0:2], high_halo, -1),
    ]
    for c in halo:
        c.start()

    def gather(group, carry):
        for u in range(unroll):
            s = group * unroll + u
            flat = index[pl.ds(s, 1), :]
            r = lax.shift_right_logical(flat, row_shift)
            c = flat & lane_mask
            hot = ones_where(iota((rows, pts), 0) == r).astype(jnp.bfloat16)
            row_hot[s] = hot
            match = iota((nz, pts), 0) == c
            col_hot[s] = ones_where(match).astype(jnp.bfloat16)
            lines = jnp.dot(
                turned[...], jnp.concatenate([hot, hot], axis=0),
                preferred_element_type=jnp.float32,
            )
            for n in range(bands):
                line = jnp.where(match, lines[n * nz : (n + 1) * nz], 0.0)
                picked[n, pl.ds(s, 1), :] = jnp.sum(line, axis=0, keepdims=True)
        return carry

    lax.fori_loop(0, slots // unroll, gather, 0)

    eye = iota((slots, slots), 0) == iota((slots, slots), 1)
    atom = jnp.sum(jnp.where(eye, slot_atom[...].astype(jnp.float32), 0.0), axis=1, keepdims=True)
    rank = atom_rank[...].astype(jnp.float32) + 1.0
    among = iota((slots, atoms_all), 1).astype(jnp.float32) == atom
    position = jnp.sum(jnp.where(among, rank, 0.0), axis=1, keepdims=True)
    spots = iota((slots, 5 * atoms_dev), 1)
    owned = spots
    for b in range(5):
        inside = (spots >= b * atoms_dev) & (spots < (b + 1) * atoms_dev)
        owned = owned + jnp.where(inside, (device(b - 2) - b) * atoms_dev, 0)
    table = ones_where((owned + 1).astype(jnp.float32) == position)

    ns, si = bands * slots, slots * nproj
    same_slot = (iota((ns, si), 0) & (slots - 1)) == lax.shift_right_logical(iota((ns, si), 1), p_bits)
    same_band = lax.shift_right_logical(iota((ns, LANES), 0), s_bits) == lax.shift_right_logical(
        iota((ns, LANES), 1), p_bits
    )
    spread = ones_where(
        ((iota((LANES, si), 0) & (nproj - 1)) == (iota((LANES, si), 1) & (nproj - 1)))
        & (iota((LANES, si), 0) < bands * nproj)
    )
    pairs = dot_dims(picked[...].reshape(ns, pts), values[...], 1, 1, HIGH)
    pairs = jnp.where(same_slot, pairs, 0.0)
    slot_rows = jnp.where(same_band, dot_dims(pairs, spread, 1, 1, HIGH), 0.0)
    coeff = jnp.sum(slot_rows.reshape(bands, slots, LANES), axis=0)
    partial = dot_dims(table, coeff, 0, 0, HIGH)
    parts[...] = partial.reshape(5, atoms_dev, LANES)

    first = [copy(2 + i, parts.at[step + 2], arrived.at[i], step) for i, step in enumerate(STEPS)]
    for c in first:
        c.start()

    def local(some):
        for n in some:
            for x in range(planes):
                f = wave[n, x]

                def plane(k):
                    if k < 0:
                        return low_halo[n, k + 2]
                    if k >= planes:
                        return high_halo[n, k - planes]
                    return wave[n, k]

                near = plane(x - 1) + plane(x + 1)
                far = plane(x - 2) + plane(x + 2)
                for axis, size in ((0, ny), (1, nz)):
                    near = near + pltpu.roll(f, 1, axis) + pltpu.roll(f, size - 1, axis)
                    far = far + pltpu.roll(f, 2, axis) + pltpu.roll(f, size - 2, axis)
                out[n, x] = (
                    (3.75 + potential[x] - energies[n]) * f - (2.0 / 3.0) * near + (1.0 / 24.0) * far
                )

    for c in halo:
        c.wait_recv()
    local(range(bands // 2))

    total = parts[2]
    for i, c in enumerate(first):
        c.wait_recv()
        total = total + arrived[i]

    nij = bands * nproj * nproj
    source, target = iota((LANES, nij), 0), iota((LANES, nij), 1)
    source_band = lax.shift_right_logical(source, p_bits)
    target_band = lax.shift_right_logical(target, 2 * p_bits)
    part_i = lax.shift_right_logical(target, p_bits) & (nproj - 1)
    part_j = target & (nproj - 1)
    source_i = source & (nproj - 1)
    by_j = ones_where((source_band == target_band) & (source_i == part_j))
    by_i = ones_where((source_band == target_band) & (source_i == part_i))
    windows[2] = dot_dims(dot(total, by_j) * effective[...], by_i, 1, 1, HIGH)

    second = [copy(6 + i, windows.at[2], windows.at[step + 2], -step) for i, step in enumerate(STEPS)]
    for c in second:
        c.start()
    local(range(bands // 2, bands))
    for c in second:
        c.wait_recv()

    slot_weight = dot(table, windows[...].reshape(5 * atoms_dev, LANES))
    slot_weight = jnp.where(same_band, jnp.concatenate([slot_weight] * bands, axis=0), 0.0)
    blocks = jnp.where(same_slot, dot(slot_weight, spread), 0.0)
    back_rows[...] = dot(blocks, values[...]).reshape(bands, slots, pts)

    acc[...] = jnp.zeros_like(acc)

    def scatter(group, carry):
        lefts, rights = [], []
        for u in range(unroll):
            s = group * unroll + u
            cols = col_hot[s].reshape(nz // 16, 16, pts)
            hot = row_hot[s]
            high_parts, low_parts = [], []
            for n in range(bands):
                line = jnp.broadcast_to(back_rows[n, pl.ds(s, 1), :], (16, pts))
                high, low = halves(line)
                high_parts.append((cols * high[None]).reshape(nz, pts))
                low_parts.append((cols * low[None]).reshape(nz, pts))
            lefts += [jnp.concatenate(high_parts, axis=0), jnp.concatenate(low_parts, axis=0)]
            rights += [hot, hot]
        acc[...] += dot_dims(jnp.concatenate(lefts, axis=1), jnp.concatenate(rights, axis=1), 1, 1)
        return carry

    lax.fori_loop(0, slots // unroll, scatter, 0)

    for n in range(bands):
        out[n] += acc[n * nz : (n + 1) * nz, :].T.reshape(planes, ny, nz)

    for c in halo + first + second:
        c.wait_send()


def per_device(
    wave, potential, energies, proj_index, proj_values, slot_atom, atom_rank, d_matrix, q_matrix
):
    bands, planes, ny, nz = wave.shape
    slots, pts = proj_index.shape
    nproj = proj_values.shape[1]
    atoms_dev = d_matrix.shape[0]
    rows = planes * ny
    effective = d_matrix[:, None] - energies[None, :, None, None] * q_matrix[:, None]
    effective = effective.reshape(atoms_dev, bands * nproj * nproj)
    f32, bf16 = jnp.float32, jnp.bfloat16
    vmem = pl.BlockSpec(memory_space=pltpu.VMEM)
    return pl.pallas_call(
        functools.partial(kernel, lax.axis_size("dom"), 2),
        out_shape=jax.ShapeDtypeStruct(wave.shape, f32),
        in_specs=[pl.BlockSpec(memory_space=pltpu.SMEM)] + [vmem] * 7,
        out_specs=vmem,
        scratch_shapes=[
            pltpu.VMEM((bands, 2, ny, nz), f32),
            pltpu.VMEM((bands, 2, ny, nz), f32),
            pltpu.VMEM((bands * nz, 2 * rows), bf16),
            pltpu.VMEM((slots, rows, pts), bf16),
            pltpu.VMEM((slots, nz, pts), bf16),
            pltpu.VMEM((bands, slots, pts), f32),
            pltpu.VMEM((bands, slots, pts), f32),
            pltpu.VMEM((bands * nz, rows), f32),
            pltpu.VMEM((5, atoms_dev, LANES), f32),
            pltpu.VMEM((4, atoms_dev, LANES), f32),
            pltpu.VMEM((5, atoms_dev, LANES), f32),
            pltpu.SemaphoreType.DMA((10,)),
            pltpu.SemaphoreType.DMA((10,)),
        ],
        compiler_params=pltpu.CompilerParams(
            collective_id=0, has_side_effects=True, vmem_limit_bytes=40 * 1024 * 1024
        ),
    )(
        energies, wave, potential, proj_index,
        proj_values.reshape(slots * nproj, pts),
        slot_atom.reshape(1, slots), atom_rank.reshape(1, -1), effective,
    )


def solution(mesh):
    placed = (
        P("band", "dom", None, None),
        P("dom", None, None),
        P("band"),
        P("dom", None),
        P("dom", None, None),
        P("dom"),
        P(),
        P("dom", None, None),
        P("dom", None, None),
    )
    return jax.shard_map(
        per_device,
        mesh=mesh,
        in_specs=placed,
        out_specs=P("band", "dom", None, None),
        check_vma=False,
    )
```

time: 158 us -> 40.4 us (0.26)
  local copies, waits for them, and re-layouts: 77.6 us -> 5.03 us
  other arithmetic: 55.4 us -> 0.01 us
  Pallas kernels: 0 us -> 35 us
  starting transfers between devices: 18.7 us -> 0 us
  matrix products: 2.96 us -> 0 us
  waiting for transfers between devices: 2.08 us -> 0 us
    scatter-add x1 -> x0, other arithmetic: 51.3 us -> none  [per_device(): result = local.reshape(bands, -1).at[:, flat_index].add(back)]
    gather x3 -> x0, local copies, waits for them, and re-layouts: 37 us -> none  [the longest x2 36.3 us: per_device(): jnp.take(center.reshape(bands, -1), flat_index, axis=1)]
    pallas_call x0 -> x1, Pallas kernels: none -> 35 us  [per_device(): pl.pallas_call(functools.partial(kernel, lax.axis_size('dom'), 2), out_sh...]
    ppermute x10 -> x0, starting transfers between devices: 18.7 us -> none  [the longest x8 16.7 us: shifted(): return lax.ppermute(value, axis, pairs)]
    reshape x4 -> x1, local copies, waits for them, and re-layouts: 13.5 us -> 0.74 us  [per_device(): atom_rank.reshape(1, -1)]
    add x1 -> x0, local copies, waits for them, and re-layouts: 8.67 us -> none  [per_device(): -0.5 * laplace_all]
    unnamed x20 -> x15, local copies, waits for them, and re-layouts: 10.9 us -> 2.56 us
    slice x10 -> x0, local copies, waits for them, and re-layouts: 6.32 us -> none  [the longest x4 3.33 us: inner_axes(): jnp.roll(field, -2, axis)]
  transfers between devices with their start and end apart: 10 -> 0, of which waited for: 2 -> 0; matrix products, arithmetic and copies ran while one was open for 7% -> 0% of each run, Pallas kernels for 0% -> 0%
where the time goes in v1:
time: 40.4 us; the launch traced here: 40.1 us
  Pallas kernels  35 us (87%)
  local copies, waits for them, and re-layouts  5.03 us (12%)
    pallas_call x1, Pallas kernels, per_device(): pl.pallas_call(functools.partial(kernel, lax.axis_size('dom'), 2), out_sh...  35 us
    unnamed x15, local copies, waits for them, and re-layouts  2.56 us
    mul x4, local copies, waits for them, and re-layouts, per_device(): energies[None, :, None, None] * q_matrix[:, None]  1.65 us

profile of v1, /device:TPU:0, one launch (start us, length us, event | category | flops | bytes accessed | tf_op | source)
XLA Modules:
  0.0 40.1 jit_solution(17907516983412596236)
XLA Ops:
  0.0 0.0 copy-start.6
  0.0 0.0 copy-start
  0.0 0.7 %reshape.18.atom_rank = s32[1,384]{1,0:T(1,128)S(1)} reshape(s32[384]{0:T(512)} %param.15) | data formatting | bytes 3072 | tf_op jit(solution)/shard_map/reshape | solution.py:266
  0.7 0.7 %mul.20 = f32[4,8,8]{2,1,0:T(8,128)S(1)} broadcast(f32[4]{0:T(128)} %energies.1), dimensions={0} | broadcast | bytes 1040 | tf_op jit(solution)/shard_map/mul | solution.py:236
  1.5 0.1 mul.21
  1.6 0.0 copy-done.6
  1.6 0.1 copy.13
  1.7 0.8 %mul.23 = f32[24,4,8,8]{0,3,2,1:T(8,128)S(1)} broadcast(f32[24,8,8]{0,2,1:T(8,128)} %param.17), dimensions={0,2,3} | broadcast | bytes 30720 | tf_op jit(solution)/shard_map/mul | solution.py:236
  2.4 0.0 copy-start.2
  2.4 0.1 copy.12
  2.5 0.0 copy-start.3
  2.5 0.0 copy-start.4
  2.5 0.0 copy-start.5
  2.5 0.0 copy-done
  2.6 0.8 %copy-done.2 = f32[4,64,128]{2,1,0:T(8,128)S(1)} copy-done((f32[4,64,128]{2,1,0:T(8,128)S(1)}, f32[4,64,128]{2,1,0:T(8,128)}, u32[]{:S(2)}) %copy-start.2) | copy-done | bytes 131096
  3.3 0.0 copy-done.3
  3.3 0.0 copy-done.4
  3.3 0.0 copy-done.5
  3.4 0.0 copy-start.1
  3.4 0.9 %copy-done.1 = f32[32,8,256]{2,1,0:T(8,128)S(1)} copy-done((f32[32,8,256]{2,1,0:T(8,128)S(1)}, f32[32,8,256]{2,1,0:T(8,128)}, u32[]{:S(2)}) %copy-start.1) | copy-done | bytes 262168
  4.3 35.0 %shard_map.91 = f32[4,4,64,128]{3,2,1,0:T(8,128)S(1)} custom-call(f32[4]{0:T(128)S(1)} %copy-done.4, f32[4,4,64,128]{3,2,1,0:T(8,128)S(1)} %copy-done, f32[4,64,128]{2,1,0:T(8,128)S(1)} %copy-done.2, s32[32,256]{1,0:T(8,128)S(1)} %copy-done.3, f32[256,256]{1,0:T(8,128)S(1)} %bitcast.4, s32[1,32]{1,0:T(1,128)S(1)} %bitcast.5, ...), custom_call_target="tpu_custom_call" | custom-call | tf_op jit(solution)/shard_map/pallas_call | solution.py:240
  39.3 0.8 %copy.15 = f32[4,4,64,128]{3,2,1,0:T(8,128)} copy(f32[4,4,64,128]{3,2,1,0:T(8,128)S(1)} %shard_map.91) | data formatting | bytes 1048576
  (2 shorter events, 0.0 us)
Async XLA Ops:
  0.0 1.6 %copy-start.6 = (f32[24,8,8]{0,2,1:T(8,128)S(1)}, f32[24,8,8]{0,2,1:T(8,128)}, u32[]{:S(2)}) copy-start(f32[24,8,8]{0,2,1:T(8,128)} %param.16) | copy-start | bytes 18436
  0.0 2.5 %copy-start = (f32[4,4,64,128]{3,2,1,0:T(8,128)S(1)}, f32[4,4,64,128]{3,2,1,0:T(8,128)}, u32[]{:S(2)}) copy-start(f32[4,4,64,128]{3,2,1,0:T(8,128)} %wave.1) | copy-start | bytes 1572868
  2.4 0.9 %copy-start.2 = (f32[4,64,128]{2,1,0:T(8,128)S(1)}, f32[4,64,128]{2,1,0:T(8,128)}, u32[]{:S(2)}) copy-start(f32[4,64,128]{2,1,0:T(8,128)} %potential.1) | copy-start | bytes 393220
  2.5 0.8 %copy-start.3 = (s32[32,256]{1,0:T(8,128)S(1)}, s32[32,256]{1,0:T(8,128)}, u32[]{:S(2)}) copy-start(s32[32,256]{1,0:T(8,128)} %index.1) | copy-start | bytes 98308
  2.5 0.8 %copy-start.4 = (f32[4]{0:T(128)S(1)}, f32[4]{0:T(128)}, u32[]{:S(2)}) copy-start(f32[4]{0:T(128)} %energies.1) | copy-start | bytes 52
  2.5 0.8 %copy-start.5 = (s32[32]{0:T(128)S(1)}, s32[32]{0:T(128)}, u32[]{:S(2)}) copy-start(s32[32]{0:T(128)} %param.14) | copy-start | bytes 388
  3.4 1.0 %copy-start.1 = (f32[32,8,256]{2,1,0:T(8,128)S(1)}, f32[32,8,256]{2,1,0:T(8,128)}, u32[]{:S(2)}) copy-start(f32[32,8,256]{2,1,0:T(8,128)} %param.13) | copy-start | bytes 786436

commit v2 on v1

--- a/solution.py
+++ b/solution.py
@@ -46,16 +46,18 @@
 
 def kernel(
     n_dom, unroll,
-    energies, wave, potential, index, values, slot_atom, atom_rank, effective,
+    energies, wave_in, potential_in, index_in, values_in, slot_atom_in, atom_rank_in, d_in, q_in,
     out,
+    wave, potential, index, values, slot_atom, atom_rank, d_part, q_part, load_sem,
     low_halo, high_halo, turned, row_hot, col_hot, picked, back_rows, acc,
     parts, arrived, windows, send_sem, recv_sem,
 ):
     bands, planes, ny, nz = wave.shape
     slots, pts = index.shape
     nproj = values.shape[0] // slots
-    atoms_dev = effective.shape[0]
-    atoms_all = atom_rank.shape[1]
+    atoms_dev = d_part.shape[2]
+    atoms_all = atom_rank.shape[0]
+    ni, ns, si = bands * nproj, bands * slots, slots * nproj
     rows = planes * ny
     wide = bands * nz
     row_shift, lane_mask = log2(nz), nz - 1
@@ -63,6 +65,17 @@
 
     me = lax.axis_index("dom")
 
+    loads = [
+        pltpu.make_async_copy(src, dst, load_sem.at[k])
+        for k, (src, dst) in enumerate((
+            (wave_in, wave), (index_in, index), (slot_atom_in, slot_atom),
+            (atom_rank_in, atom_rank), (values_in, values), (d_in, d_part), (q_in, q_part),
+            (potential_in, potential),
+        ))
+    ]
+    for c in loads:
+        c.start()
+
     def device(step):
         return lax.rem(me + step + n_dom, n_dom)
 
@@ -70,11 +83,28 @@
     for step in STEPS:
         pl.semaphore_signal(barrier, inc=1, device_id={"dom": device(step)}, device_id_type=MESH)
 
+    loads[0].wait()
     for n in range(bands):
         block = wave[n].reshape(rows, nz).T
         high, low = halves(block)
         turned[n * nz : (n + 1) * nz, :rows] = high
         turned[n * nz : (n + 1) * nz, rows:] = low
+
+    eye = iota((slots, slots), 0) == iota((slots, slots), 1)
+    for c in loads[1:4]:
+        c.wait()
+    atom = jnp.sum(jnp.where(eye, slot_atom[...].astype(jnp.float32), 0.0), axis=1, keepdims=True)
+    rank = atom_rank[...].astype(jnp.float32).reshape(1, atoms_all) + 1.0
+    among = iota((slots, atoms_all), 1).astype(jnp.float32) == atom
+    position = jnp.sum(jnp.where(among, rank, 0.0), axis=1, keepdims=True)
+    place = iota((slots, LANES), 1)
+    tables = []
+    for b in range(5):
+        owned = (place + device(b - 2) * atoms_dev + 1).astype(jnp.float32)
+        tables.append(ones_where((owned == position) & (place < atoms_dev)))
+    table = jnp.concatenate(tables, axis=1)
+    windows[2] = jnp.zeros_like(windows[2])
+    acc[...] = jnp.zeros_like(acc)
 
     pl.semaphore_wait(barrier, len(STEPS))
 
@@ -112,33 +142,19 @@
 
     lax.fori_loop(0, slots // unroll, gather, 0)
 
-    eye = iota((slots, slots), 0) == iota((slots, slots), 1)
-    atom = jnp.sum(jnp.where(eye, slot_atom[...].astype(jnp.float32), 0.0), axis=1, keepdims=True)
-    rank = atom_rank[...].astype(jnp.float32) + 1.0
-    among = iota((slots, atoms_all), 1).astype(jnp.float32) == atom
-    position = jnp.sum(jnp.where(among, rank, 0.0), axis=1, keepdims=True)
-    spots = iota((slots, 5 * atoms_dev), 1)
-    owned = spots
-    for b in range(5):
-        inside = (spots >= b * atoms_dev) & (spots < (b + 1) * atoms_dev)
-        owned = owned + jnp.where(inside, (device(b - 2) - b) * atoms_dev, 0)
-    table = ones_where((owned + 1).astype(jnp.float32) == position)
-
-    ns, si = bands * slots, slots * nproj
+    loads[4].wait()
     same_slot = (iota((ns, si), 0) & (slots - 1)) == lax.shift_right_logical(iota((ns, si), 1), p_bits)
-    same_band = lax.shift_right_logical(iota((ns, LANES), 0), s_bits) == lax.shift_right_logical(
-        iota((ns, LANES), 1), p_bits
-    )
-    spread = ones_where(
-        ((iota((LANES, si), 0) & (nproj - 1)) == (iota((LANES, si), 1) & (nproj - 1)))
-        & (iota((LANES, si), 0) < bands * nproj)
-    )
+    same_band = lax.shift_right_logical(iota((ns, ni), 0), s_bits) == lax.shift_right_logical(
+        iota((ns, ni), 1), p_bits
+    )
+    spread = ones_where((iota((ni, si), 0) & (nproj - 1)) == (iota((ni, si), 1) & (nproj - 1)))
     pairs = dot_dims(picked[...].reshape(ns, pts), values[...], 1, 1, HIGH)
     pairs = jnp.where(same_slot, pairs, 0.0)
     slot_rows = jnp.where(same_band, dot_dims(pairs, spread, 1, 1, HIGH), 0.0)
-    coeff = jnp.sum(slot_rows.reshape(bands, slots, LANES), axis=0)
-    partial = dot_dims(table, coeff, 0, 0, HIGH)
-    parts[...] = partial.reshape(5, atoms_dev, LANES)
+    coeff = jnp.sum(slot_rows.reshape(bands, slots, ni), axis=0)
+    partial = dot_dims(coeff, table, 0, 0, HIGH)
+    for b in range(5):
+        parts[b] = partial[:, b * LANES : (b + 1) * LANES]
 
     first = [copy(2 + i, parts.at[step + 2], arrived.at[i], step) for i, step in enumerate(STEPS)]
     for c in first:
@@ -165,6 +181,7 @@
                     (3.75 + potential[x] - energies[n]) * f - (2.0 / 3.0) * near + (1.0 / 24.0) * far
                 )
 
+    loads[7].wait()
     for c in halo:
         c.wait_recv()
     local(range(bands // 2))
@@ -174,16 +191,12 @@
         c.wait_recv()
         total = total + arrived[i]
 
-    nij = bands * nproj * nproj
-    source, target = iota((LANES, nij), 0), iota((LANES, nij), 1)
-    source_band = lax.shift_right_logical(source, p_bits)
-    target_band = lax.shift_right_logical(target, 2 * p_bits)
-    part_i = lax.shift_right_logical(target, p_bits) & (nproj - 1)
-    part_j = target & (nproj - 1)
-    source_i = source & (nproj - 1)
-    by_j = ones_where((source_band == target_band) & (source_i == part_j))
-    by_i = ones_where((source_band == target_band) & (source_i == part_i))
-    windows[2] = dot_dims(dot(total, by_j) * effective[...], by_i, 1, 1, HIGH)
+    for c in loads[5:7]:
+        c.wait()
+    for n in range(bands):
+        matrix = d_part[...] - energies[n] * q_part[...]
+        column = total[n * nproj : (n + 1) * nproj, :atoms_dev]
+        windows[2, n * nproj : (n + 1) * nproj, :atoms_dev] = jnp.sum(matrix * column[None], axis=1)
 
     second = [copy(6 + i, windows.at[2], windows.at[step + 2], -step) for i, step in enumerate(STEPS)]
     for c in second:
@@ -192,12 +205,11 @@
     for c in second:
         c.wait_recv()
 
-    slot_weight = dot(table, windows[...].reshape(5 * atoms_dev, LANES))
+    around = jnp.concatenate([windows[b] for b in range(5)], axis=1)
+    slot_weight = dot_dims(table, around, 1, 1, HIGH)
     slot_weight = jnp.where(same_band, jnp.concatenate([slot_weight] * bands, axis=0), 0.0)
     blocks = jnp.where(same_slot, dot(slot_weight, spread), 0.0)
     back_rows[...] = dot(blocks, values[...]).reshape(bands, slots, pts)
-
-    acc[...] = jnp.zeros_like(acc)
 
     def scatter(group, carry):
         lefts, rights = [], []
@@ -232,17 +244,27 @@
     slots, pts = proj_index.shape
     nproj = proj_values.shape[1]
     atoms_dev = d_matrix.shape[0]
+    assert atoms_dev <= LANES
     rows = planes * ny
-    effective = d_matrix[:, None] - energies[None, :, None, None] * q_matrix[:, None]
-    effective = effective.reshape(atoms_dev, bands * nproj * nproj)
     f32, bf16 = jnp.float32, jnp.bfloat16
     vmem = pl.BlockSpec(memory_space=pltpu.VMEM)
+    atom_block = (bands * nproj, LANES)
     return pl.pallas_call(
-        functools.partial(kernel, lax.axis_size("dom"), 2),
+        functools.partial(kernel, lax.axis_size("dom"), 4),
         out_shape=jax.ShapeDtypeStruct(wave.shape, f32),
-        in_specs=[pl.BlockSpec(memory_space=pltpu.SMEM)] + [vmem] * 7,
+        in_specs=[pl.BlockSpec(memory_space=pltpu.SMEM)]
+        + [pl.BlockSpec(memory_space=pltpu.HBM)] * 8,
         out_specs=vmem,
         scratch_shapes=[
+            pltpu.VMEM(wave.shape, f32),
+            pltpu.VMEM(potential.shape, f32),
+            pltpu.VMEM(proj_index.shape, jnp.int32),
+            pltpu.VMEM((slots * nproj, pts), f32),
+            pltpu.VMEM((1, slots), jnp.int32),
+            pltpu.VMEM(atom_rank.shape, jnp.int32),
+            pltpu.VMEM((nproj, nproj, atoms_dev), f32),
+            pltpu.VMEM((nproj, nproj, atoms_dev), f32),
+            pltpu.SemaphoreType.DMA((8,)),
             pltpu.VMEM((bands, 2, ny, nz), f32),
             pltpu.VMEM((bands, 2, ny, nz), f32),
             pltpu.VMEM((bands * nz, 2 * rows), bf16),
@@ -251,19 +273,20 @@
             pltpu.VMEM((bands, slots, pts), f32),
             pltpu.VMEM((bands, slots, pts), f32),
             pltpu.VMEM((bands * nz, rows), f32),
-            pltpu.VMEM((5, atoms_dev, LANES), f32),
-            pltpu.VMEM((4, atoms_dev, LANES), f32),
-            pltpu.VMEM((5, atoms_dev, LANES), f32),
+            pltpu.VMEM((5,) + atom_block, f32),
+            pltpu.VMEM((4,) + atom_block, f32),
+            pltpu.VMEM((5,) + atom_block, f32),
             pltpu.SemaphoreType.DMA((10,)),
             pltpu.SemaphoreType.DMA((10,)),
         ],
         compiler_params=pltpu.CompilerParams(
-            collective_id=0, has_side_effects=True, vmem_limit_bytes=40 * 1024 * 1024
+            collective_id=0, has_side_effects=True, vmem_limit_bytes=60 * 1024 * 1024
         ),
     )(
         energies, wave, potential, proj_index,
         proj_values.reshape(slots * nproj, pts),
-        slot_atom.reshape(1, slots), atom_rank.reshape(1, -1), effective,
+        slot_atom.reshape(1, slots), atom_rank,
+        jnp.transpose(d_matrix, (1, 2, 0)), jnp.transpose(q_matrix, (1, 2, 0)),
     )
 
 

time: 40.4 us -> 35 us (0.87)
  local copies, waits for them, and re-layouts: 5.03 us -> 1.89 us
  Pallas kernels: 35 us -> 32.9 us
    pallas_call x1, Pallas kernels: 35 us -> 32.9 us  [per_device(): pl.pallas_call(functools.partial(kernel, lax.axis_size('dom'), 4), out_sh...]
    mul x4 -> x0, local copies, waits for them, and re-layouts: 1.65 us -> none  [per_device(): energies[None, :, None, None] * q_matrix[:, None]]
    reshape x1 -> x0, local copies, waits for them, and re-layouts: 0.74 us -> none  [per_device(): atom_rank.reshape(1, -1)]
    unnamed x15 -> x1, local copies, waits for them, and re-layouts: 2.56 us -> 1.89 us
where the time goes in v2:
time: 35 us; the launch traced here: 34.8 us
  Pallas kernels  32.9 us (94%)
  local copies, waits for them, and re-layouts  1.89 us (5%)
    pallas_call x1, Pallas kernels, per_device(): pl.pallas_call(functools.partial(kernel, lax.axis_size('dom'), 4), out_sh...  32.9 us
    unnamed x1, local copies, waits for them, and re-layouts  1.89 us

profile of v2, /device:TPU:0, one launch (start us, length us, event | category | flops | bytes accessed | tf_op | source)
XLA Modules:
  0.0 34.8 jit_solution(16189893497176454247)
XLA Ops:
  0.0 32.9 %shard_map.91 = f32[4,4,64,128]{3,2,1,0:T(8,128)} custom-call(f32[4]{0:T(128)} %energies.1, f32[4,4,64,128]{3,2,1,0:T(8,128)} %wave_in.1, f32[4,64,128]{2,1,0:T(8,128)} %potential_in.1, s32[32,256]{1,0:T(8,128)} %index_in.1, f32[256,256]{1,0:T(8,128)} %bitcast.4, s32[1,32]{1,0:T(1,128)} %bitcast.7, s32[384]{0:T(512)} %atom_rank_in.1, f32[8,8,24]{2,1,0:T(8,128)} %bitcast.5, ...), custom_call_target="tpu_custom_call" | custom-call | tf_op jit(solution)/shard_map/pallas_call | solution.py:252
  32.9 1.9 %copy.11 = f32[4,4,64,128]{3,2,1,0:T(8,128)} copy(f32[4,4,64,128]{3,2,1,0:T(8,128)} %shard_map.91) | data formatting | bytes 1048576

commit v3 on v2

--- a/solution.py
+++ b/solution.py
@@ -7,7 +7,6 @@
 from jax.experimental.pallas import tpu as pltpu
 from jax.sharding import PartitionSpec as P
 
-HIGH = lax.Precision.HIGHEST
 MESH = pl.DeviceIdType.MESH
 STEPS = (-2, -1, 1, 2)
 LANES = 128
@@ -27,14 +26,24 @@
     return jnp.where(mask, 1.0, 0.0).astype(jnp.float32)
 
 
-def dot(a, b):
-    return jnp.dot(a, b, precision=HIGH, preferred_element_type=jnp.float32)
-
-
-def dot_dims(a, b, left, right, precision=None):
+def dot_dims(a, b, left, right):
     return lax.dot_general(
-        a, b, (((left,), (right,)), ((), ())),
-        precision=precision, preferred_element_type=jnp.float32,
+        a, b, (((left,), (right,)), ((), ())), preferred_element_type=jnp.float32
+    )
+
+
+def dot_hot(a, hot, left, right):
+    high, low = halves(a)
+    hot = hot.astype(jnp.bfloat16)
+    return dot_dims(high, hot, left, right) + dot_dims(low, hot, left, right)
+
+
+def dot_full(a, b, left, right):
+    (a_high, a_low), (b_high, b_low) = halves(a), halves(b)
+    return (
+        dot_dims(a_high, b_high, left, right)
+        + dot_dims(a_high, b_low, left, right)
+        + dot_dims(a_low, b_high, left, right)
     )
 
 
@@ -49,7 +58,7 @@
     energies, wave_in, potential_in, index_in, values_in, slot_atom_in, atom_rank_in, d_in, q_in,
     out,
     wave, potential, index, values, slot_atom, atom_rank, d_part, q_part, load_sem,
-    low_halo, high_halo, turned, row_hot, col_hot, picked, back_rows, acc,
+    low_halo, high_halo, row_hot, col_hot, picked, back_rows, acc,
     parts, arrived, windows, send_sem, recv_sem,
 ):
     bands, planes, ny, nz = wave.shape
@@ -82,13 +91,6 @@
     barrier = pltpu.get_barrier_semaphore()
     for step in STEPS:
         pl.semaphore_signal(barrier, inc=1, device_id={"dom": device(step)}, device_id_type=MESH)
-
-    loads[0].wait()
-    for n in range(bands):
-        block = wave[n].reshape(rows, nz).T
-        high, low = halves(block)
-        turned[n * nz : (n + 1) * nz, :rows] = high
-        turned[n * nz : (n + 1) * nz, rows:] = low
 
     eye = iota((slots, slots), 0) == iota((slots, slots), 1)
     for c in loads[1:4]:
@@ -106,6 +108,7 @@
     windows[2] = jnp.zeros_like(windows[2])
     acc[...] = jnp.zeros_like(acc)
 
+    loads[0].wait()
     pl.semaphore_wait(barrier, len(STEPS))
 
     def copy(k, src, dst, step):
@@ -121,26 +124,34 @@
     for c in halo:
         c.start()
 
-    def gather(group, carry):
-        for u in range(unroll):
-            s = group * unroll + u
-            flat = index[pl.ds(s, 1), :]
-            r = lax.shift_right_logical(flat, row_shift)
-            c = flat & lane_mask
-            hot = ones_where(iota((rows, pts), 0) == r).astype(jnp.bfloat16)
-            row_hot[s] = hot
-            match = iota((nz, pts), 0) == c
-            col_hot[s] = ones_where(match).astype(jnp.bfloat16)
-            lines = jnp.dot(
-                turned[...], jnp.concatenate([hot, hot], axis=0),
-                preferred_element_type=jnp.float32,
-            )
-            for n in range(bands):
-                line = jnp.where(match, lines[n * nz : (n + 1) * nz], 0.0)
-                picked[n, pl.ds(s, 1), :] = jnp.sum(line, axis=0, keepdims=True)
-        return carry
-
-    lax.fori_loop(0, slots // unroll, gather, 0)
+    tiles = [slice(k * LANES, (k + 1) * LANES) for k in range(pts // LANES)]
+    at_row = lax.shift_right_logical(index[...], row_shift)
+    at_col = index[...] & lane_mask
+    row_tiles = [at_row[:, t] for t in tiles]
+    col_tiles = [at_col[:, t] for t in tiles]
+
+    for pair in range(0, bands, 2):
+        pair_bands = range(pair, min(pair + 2, bands))
+
+        def gather(group, found):
+            x, y = group // (ny // 8), lax.rem(group, ny // 8) * 8
+            blocks = [wave[n, x, pl.ds(pl.multiple_of(y, 8), 8), :] for n in pair_bands]
+            found = list(found)
+            for u in range(8):
+                here = [r == group * 8 + u for r in row_tiles]
+                k = 0
+                for block in blocks:
+                    row = jnp.broadcast_to(block[u : u + 1], (slots, LANES))
+                    for match, c in zip(here, col_tiles):
+                        line = jnp.take_along_axis(row, c, axis=1, mode="promise_in_bounds")
+                        found[k] = jnp.where(match, line, found[k])
+                        k += 1
+            return tuple(found)
+
+        zero = jnp.zeros((slots, LANES), jnp.float32)
+        found = lax.fori_loop(0, rows // 8, gather, (zero,) * (len(pair_bands) * len(tiles)))
+        for k, line in enumerate(found):
+            picked[pair + k // len(tiles), :, tiles[k % len(tiles)]] = line
 
     loads[4].wait()
     same_slot = (iota((ns, si), 0) & (slots - 1)) == lax.shift_right_logical(iota((ns, si), 1), p_bits)
@@ -148,11 +159,11 @@
         iota((ns, ni), 1), p_bits
     )
     spread = ones_where((iota((ni, si), 0) & (nproj - 1)) == (iota((ni, si), 1) & (nproj - 1)))
-    pairs = dot_dims(picked[...].reshape(ns, pts), values[...], 1, 1, HIGH)
+    pairs = dot_full(picked[...].reshape(ns, pts), values[...], 1, 1)
     pairs = jnp.where(same_slot, pairs, 0.0)
-    slot_rows = jnp.where(same_band, dot_dims(pairs, spread, 1, 1, HIGH), 0.0)
+    slot_rows = jnp.where(same_band, dot_hot(pairs, spread, 1, 1), 0.0)
     coeff = jnp.sum(slot_rows.reshape(bands, slots, ni), axis=0)
-    partial = dot_dims(coeff, table, 0, 0, HIGH)
+    partial = dot_hot(coeff.T, table, 1, 0)
     for b in range(5):
         parts[b] = partial[:, b * LANES : (b + 1) * LANES]
 
@@ -181,6 +192,15 @@
                     (3.75 + potential[x] - energies[n]) * f - (2.0 / 3.0) * near + (1.0 / 24.0) * far
                 )
 
+    def hots(s, carry):
+        flat = index[pl.ds(s, 1), :]
+        row_hot[s] = ones_where(
+            iota((rows, pts), 0) == lax.shift_right_logical(flat, row_shift)
+        ).astype(jnp.bfloat16)
+        col_hot[s] = ones_where(iota((nz, pts), 0) == (flat & lane_mask)).astype(jnp.bfloat16)
+        return carry
+
+    lax.fori_loop(0, slots // 2, hots, 0)
     loads[7].wait()
     for c in halo:
         c.wait_recv()
@@ -201,37 +221,38 @@
     second = [copy(6 + i, windows.at[2], windows.at[step + 2], -step) for i, step in enumerate(STEPS)]
     for c in second:
         c.start()
+    lax.fori_loop(slots // 2, slots, hots, 0)
     local(range(bands // 2, bands))
     for c in second:
         c.wait_recv()
 
     around = jnp.concatenate([windows[b] for b in range(5)], axis=1)
-    slot_weight = dot_dims(table, around, 1, 1, HIGH)
+    slot_weight = dot_hot(around, table, 1, 1).T
     slot_weight = jnp.where(same_band, jnp.concatenate([slot_weight] * bands, axis=0), 0.0)
-    blocks = jnp.where(same_slot, dot(slot_weight, spread), 0.0)
-    back_rows[...] = dot(blocks, values[...]).reshape(bands, slots, pts)
+    blocks = jnp.where(same_slot, dot_hot(slot_weight, spread, 1, 0), 0.0)
+    back_rows[...] = dot_full(blocks, values[...], 1, 0).reshape(bands, slots, pts)
 
     def scatter(group, carry):
         lefts, rights = [], []
         for u in range(unroll):
             s = group * unroll + u
             cols = col_hot[s].reshape(nz // 16, 16, pts)
-            hot = row_hot[s]
             high_parts, low_parts = [], []
             for n in range(bands):
                 line = jnp.broadcast_to(back_rows[n, pl.ds(s, 1), :], (16, pts))
                 high, low = halves(line)
                 high_parts.append((cols * high[None]).reshape(nz, pts))
                 low_parts.append((cols * low[None]).reshape(nz, pts))
-            lefts += [jnp.concatenate(high_parts, axis=0), jnp.concatenate(low_parts, axis=0)]
-            rights += [hot, hot]
+            lefts.append(jnp.concatenate(high_parts + low_parts, axis=0))
+            rights.append(row_hot[s])
         acc[...] += dot_dims(jnp.concatenate(lefts, axis=1), jnp.concatenate(rights, axis=1), 1, 1)
         return carry
 
     lax.fori_loop(0, slots // unroll, scatter, 0)
 
     for n in range(bands):
-        out[n] += acc[n * nz : (n + 1) * nz, :].T.reshape(planes, ny, nz)
+        added = acc[n * nz : (n + 1) * nz, :] + acc[wide + n * nz : wide + (n + 1) * nz, :]
+        out[n] += added.T.reshape(planes, ny, nz)
 
     for c in halo + first + second:
         c.wait_send()
@@ -244,7 +265,7 @@
     slots, pts = proj_index.shape
     nproj = proj_values.shape[1]
     atoms_dev = d_matrix.shape[0]
-    assert atoms_dev <= LANES
+    assert atoms_dev <= LANES and nz == LANES
     rows = planes * ny
     f32, bf16 = jnp.float32, jnp.bfloat16
     vmem = pl.BlockSpec(memory_space=pltpu.VMEM)
@@ -267,12 +288,11 @@
             pltpu.SemaphoreType.DMA((8,)),
             pltpu.VMEM((bands, 2, ny, nz), f32),
             pltpu.VMEM((bands, 2, ny, nz), f32),
-            pltpu.VMEM((bands * nz, 2 * rows), bf16),
             pltpu.VMEM((slots, rows, pts), bf16),
             pltpu.VMEM((slots, nz, pts), bf16),
             pltpu.VMEM((bands, slots, pts), f32),
             pltpu.VMEM((bands, slots, pts), f32),
-            pltpu.VMEM((bands * nz, rows), f32),
+            pltpu.VMEM((2 * bands * nz, rows), f32),
             pltpu.VMEM((5,) + atom_block, f32),
             pltpu.VMEM((4,) + atom_block, f32),
             pltpu.VMEM((5,) + atom_block, f32),

time: 35 us -> 55 us (1.57)
  Pallas kernels: 32.9 us -> 52.9 us
    pallas_call x1, Pallas kernels: 32.9 us -> 52.9 us  [per_device(): pl.pallas_call(functools.partial(kernel, lax.axis_size('dom'), 4), out_sh...]
where the time goes in v3:
time: 55 us; the launch traced here: 54.8 us
  Pallas kernels  52.9 us (96%)
  local copies, waits for them, and re-layouts  1.89 us (3%)
    pallas_call x1, Pallas kernels, per_device(): pl.pallas_call(functools.partial(kernel, lax.axis_size('dom'), 4), out_sh...  52.9 us
    unnamed x1, local copies, waits for them, and re-layouts  1.89 us

profile of v3, /device:TPU:0, one launch (start us, length us, event | category | flops | bytes accessed | tf_op | source)
XLA Modules:
  0.0 54.8 jit_solution(17248781036178543614)
XLA Ops:
  0.0 52.9 %shard_map.91 = f32[4,4,64,128]{3,2,1,0:T(8,128)} custom-call(f32[4]{0:T(128)} %energies.1, f32[4,4,64,128]{3,2,1,0:T(8,128)} %wave_in.1, f32[4,64,128]{2,1,0:T(8,128)} %potential_in.1, s32[32,256]{1,0:T(8,128)} %index_in.1, f32[256,256]{1,0:T(8,128)} %bitcast.4, s32[1,32]{1,0:T(1,128)} %bitcast.7, s32[384]{0:T(512)} %atom_rank_in.1, f32[8,8,24]{2,1,0:T(8,128)} %bitcast.5, ...), custom_call_target="tpu_custom_call" | custom-call | tf_op jit(solution)/shard_map/pallas_call | solution.py:273
  52.9 1.9 %copy.11 = f32[4,4,64,128]{3,2,1,0:T(8,128)} copy(f32[4,4,64,128]{3,2,1,0:T(8,128)} %shard_map.91) | data formatting | bytes 1048576

commit v4 on v3

--- a/solution.py
+++ b/solution.py
@@ -58,7 +58,7 @@
     energies, wave_in, potential_in, index_in, values_in, slot_atom_in, atom_rank_in, d_in, q_in,
     out,
     wave, potential, index, values, slot_atom, atom_rank, d_part, q_part, load_sem,
-    low_halo, high_halo, row_hot, col_hot, picked, back_rows, acc,
+    low_halo, high_halo, turned, row_hot, col_hot, picked, back_rows, acc,
     parts, arrived, windows, send_sem, recv_sem,
 ):
     bands, planes, ny, nz = wave.shape
@@ -124,34 +124,29 @@
     for c in halo:
         c.start()
 
-    tiles = [slice(k * LANES, (k + 1) * LANES) for k in range(pts // LANES)]
-    at_row = lax.shift_right_logical(index[...], row_shift)
-    at_col = index[...] & lane_mask
-    row_tiles = [at_row[:, t] for t in tiles]
-    col_tiles = [at_col[:, t] for t in tiles]
-
-    for pair in range(0, bands, 2):
-        pair_bands = range(pair, min(pair + 2, bands))
-
-        def gather(group, found):
-            x, y = group // (ny // 8), lax.rem(group, ny // 8) * 8
-            blocks = [wave[n, x, pl.ds(pl.multiple_of(y, 8), 8), :] for n in pair_bands]
-            found = list(found)
-            for u in range(8):
-                here = [r == group * 8 + u for r in row_tiles]
-                k = 0
-                for block in blocks:
-                    row = jnp.broadcast_to(block[u : u + 1], (slots, LANES))
-                    for match, c in zip(here, col_tiles):
-                        line = jnp.take_along_axis(row, c, axis=1, mode="promise_in_bounds")
-                        found[k] = jnp.where(match, line, found[k])
-                        k += 1
-            return tuple(found)
-
-        zero = jnp.zeros((slots, LANES), jnp.float32)
-        found = lax.fori_loop(0, rows // 8, gather, (zero,) * (len(pair_bands) * len(tiles)))
-        for k, line in enumerate(found):
-            picked[pair + k // len(tiles), :, tiles[k % len(tiles)]] = line
+    for n in range(bands):
+        high, low = halves(wave[n].reshape(rows, nz).T)
+        turned[n * nz : (n + 1) * nz, :] = high
+        turned[wide + n * nz : wide + (n + 1) * nz, :] = low
+
+    def gather(group, carry):
+        for u in range(unroll):
+            s = group * unroll + u
+            flat = index[pl.ds(s, 1), :]
+            hot = ones_where(
+                iota((rows, pts), 0) == lax.shift_right_logical(flat, row_shift)
+            ).astype(jnp.bfloat16)
+            row_hot[s] = hot
+            match = iota((nz, pts), 0) == (flat & lane_mask)
+            col_hot[s] = ones_where(match).astype(jnp.bfloat16)
+            lines = dot_dims(turned[...], hot, 1, 0)
+            for n in range(bands):
+                line = lines[n * nz : (n + 1) * nz] + lines[wide + n * nz : wide + (n + 1) * nz]
+                line = jnp.where(match, line, 0.0)
+                picked[n, pl.ds(s, 1), :] = jnp.sum(line, axis=0, keepdims=True)
+        return carry
+
+    lax.fori_loop(0, slots // unroll, gather, 0)
 
     loads[4].wait()
     same_slot = (iota((ns, si), 0) & (slots - 1)) == lax.shift_right_logical(iota((ns, si), 1), p_bits)
@@ -192,15 +187,6 @@
                     (3.75 + potential[x] - energies[n]) * f - (2.0 / 3.0) * near + (1.0 / 24.0) * far
                 )
 
-    def hots(s, carry):
-        flat = index[pl.ds(s, 1), :]
-        row_hot[s] = ones_where(
-            iota((rows, pts), 0) == lax.shift_right_logical(flat, row_shift)
-        ).astype(jnp.bfloat16)
-        col_hot[s] = ones_where(iota((nz, pts), 0) == (flat & lane_mask)).astype(jnp.bfloat16)
-        return carry
-
-    lax.fori_loop(0, slots // 2, hots, 0)
     loads[7].wait()
     for c in halo:
         c.wait_recv()
@@ -221,7 +207,6 @@
     second = [copy(6 + i, windows.at[2], windows.at[step + 2], -step) for i, step in enumerate(STEPS)]
     for c in second:
         c.start()
-    lax.fori_loop(slots // 2, slots, hots, 0)
     local(range(bands // 2, bands))
     for c in second:
         c.wait_recv()
@@ -288,6 +273,7 @@
             pltpu.SemaphoreType.DMA((8,)),
             pltpu.VMEM((bands, 2, ny, nz), f32),
             pltpu.VMEM((bands, 2, ny, nz), f32),
+            pltpu.VMEM((2 * bands * nz, rows), bf16),
             pltpu.VMEM((slots, rows, pts), bf16),
             pltpu.VMEM((slots, nz, pts), bf16),
             pltpu.VMEM((bands, slots, pts), f32),

time: 55 us -> 34.2 us (0.62)
  Pallas kernels: 52.9 us -> 32.1 us
    pallas_call x1, Pallas kernels: 52.9 us -> 32.1 us  [per_device(): pl.pallas_call(functools.partial(kernel, lax.axis_size('dom'), 4), out_sh...]
where the time goes in v4:
time: 34.2 us; the launch traced here: 34 us
  Pallas kernels  32.1 us (94%)
  local copies, waits for them, and re-layouts  1.89 us (6%)
    pallas_call x1, Pallas kernels, per_device(): pl.pallas_call(functools.partial(kernel, lax.axis_size('dom'), 4), out_sh...  32.1 us
    unnamed x1, local copies, waits for them, and re-layouts  1.89 us

profile of v4, /device:TPU:0, one launch (start us, length us, event | category | flops | bytes accessed | tf_op | source)
XLA Modules:
  0.0 34.0 jit_solution(12042275867639983729)
XLA Ops:
  0.0 32.1 %shard_map.91 = f32[4,4,64,128]{3,2,1,0:T(8,128)} custom-call(f32[4]{0:T(128)} %energies.1, f32[4,4,64,128]{3,2,1,0:T(8,128)} %wave_in.1, f32[4,64,128]{2,1,0:T(8,128)} %potential_in.1, s32[32,256]{1,0:T(8,128)} %index_in.1, f32[256,256]{1,0:T(8,128)} %bitcast.4, s32[1,32]{1,0:T(1,128)} %bitcast.7, s32[384]{0:T(512)} %atom_rank_in.1, f32[8,8,24]{2,1,0:T(8,128)} %bitcast.5, ...), custom_call_target="tpu_custom_call" | custom-call | tf_op jit(solution)/shard_map/pallas_call | solution.py:258
  32.1 1.9 %copy.11 = f32[4,4,64,128]{3,2,1,0:T(8,128)} copy(f32[4,4,64,128]{3,2,1,0:T(8,128)} %shard_map.91) | data formatting | bytes 1048576

commit v5 on v4

--- a/solution.py
+++ b/solution.py
@@ -136,7 +136,6 @@
             hot = ones_where(
                 iota((rows, pts), 0) == lax.shift_right_logical(flat, row_shift)
             ).astype(jnp.bfloat16)
-            row_hot[s] = hot
             match = iota((nz, pts), 0) == (flat & lane_mask)
             col_hot[s] = ones_where(match).astype(jnp.bfloat16)
             lines = dot_dims(turned[...], hot, 1, 0)
@@ -166,30 +165,39 @@
     for c in first:
         c.start()
 
+    by_slot = lax.shift_right_logical(index[...], row_shift).astype(jnp.float32).T
+    by_slot = by_slot.astype(jnp.bfloat16)
+
+    def hots(group, carry):
+        for u in range(unroll):
+            s = group * unroll + u
+            chosen = ones_where(iota((slots, rows), 0) == s).astype(jnp.bfloat16)
+            spread_rows = dot_dims(by_slot, chosen, 1, 0)
+            match = spread_rows == iota((pts, rows), 1).astype(jnp.float32)
+            row_hot[s] = ones_where(match).astype(jnp.bfloat16)
+        return carry
+
     def local(some):
         for n in some:
             for x in range(planes):
                 f = wave[n, x]
-
-                def plane(k):
-                    if k < 0:
-                        return low_halo[n, k + 2]
-                    if k >= planes:
-                        return high_halo[n, k - planes]
-                    return wave[n, k]
-
-                near = plane(x - 1) + plane(x + 1)
-                far = plane(x - 2) + plane(x + 2)
+                near, far = jnp.zeros_like(f), jnp.zeros_like(f)
                 for axis, size in ((0, ny), (1, nz)):
                     near = near + pltpu.roll(f, 1, axis) + pltpu.roll(f, size - 1, axis)
                     far = far + pltpu.roll(f, 2, axis) + pltpu.roll(f, size - 2, axis)
+                for k in (x - 1, x + 1):
+                    if 0 <= k < planes:
+                        near = near + wave[n, k]
+                for k in (x - 2, x + 2):
+                    if 0 <= k < planes:
+                        far = far + wave[n, k]
                 out[n, x] = (
                     (3.75 + potential[x] - energies[n]) * f - (2.0 / 3.0) * near + (1.0 / 24.0) * far
                 )
 
+    half = slots // unroll // 2
+    lax.fori_loop(0, half, hots, 0)
     loads[7].wait()
-    for c in halo:
-        c.wait_recv()
     local(range(bands // 2))
 
     total = parts[2]
@@ -207,6 +215,7 @@
     second = [copy(6 + i, windows.at[2], windows.at[step + 2], -step) for i, step in enumerate(STEPS)]
     for c in second:
         c.start()
+    lax.fori_loop(half, slots // unroll, hots, 0)
     local(range(bands // 2, bands))
     for c in second:
         c.wait_recv()
@@ -230,14 +239,27 @@
                 low_parts.append((cols * low[None]).reshape(nz, pts))
             lefts.append(jnp.concatenate(high_parts + low_parts, axis=0))
             rights.append(row_hot[s])
-        acc[...] += dot_dims(jnp.concatenate(lefts, axis=1), jnp.concatenate(rights, axis=1), 1, 1)
+        acc[...] += dot_dims(jnp.concatenate(lefts, axis=1), jnp.concatenate(rights, axis=0), 1, 0)
         return carry
 
     lax.fori_loop(0, slots // unroll, scatter, 0)
+
+    for c in halo:
+        c.wait_recv()
+
+    def beyond(n, k):
+        return low_halo[n, k + 2] if k < 0 else high_halo[n, k - planes]
 
     for n in range(bands):
         added = acc[n * nz : (n + 1) * nz, :] + acc[wide + n * nz : wide + (n + 1) * nz, :]
-        out[n] += added.T.reshape(planes, ny, nz)
+        added = added.T.reshape(planes, ny, nz)
+        for x in range(planes):
+            plane = out[n, x] + added[x]
+            for distance, factor in ((1, -2.0 / 3.0), (2, 1.0 / 24.0)):
+                for k in (x - distance, x + distance):
+                    if not 0 <= k < planes:
+                        plane = plane + factor * beyond(n, k)
+            out[n, x] = plane
 
     for c in halo + first + second:
         c.wait_send()
@@ -274,7 +296,7 @@
             pltpu.VMEM((bands, 2, ny, nz), f32),
             pltpu.VMEM((bands, 2, ny, nz), f32),
             pltpu.VMEM((2 * bands * nz, rows), bf16),
-            pltpu.VMEM((slots, rows, pts), bf16),
+            pltpu.VMEM((slots, pts, rows), bf16),
             pltpu.VMEM((slots, nz, pts), bf16),
             pltpu.VMEM((bands, slots, pts), f32),
             pltpu.VMEM((bands, slots, pts), f32),

time: 34.2 us -> 33.9 us (level)
  no operation moved by 1% of the time
where the time goes in v5:
time: 33.9 us; the launch traced here: 33.7 us
  Pallas kernels  31.9 us (94%)
  local copies, waits for them, and re-layouts  1.89 us (6%)
    pallas_call x1, Pallas kernels, per_device(): pl.pallas_call(functools.partial(kernel, lax.axis_size('dom'), 4), out_sh...  31.9 us
    unnamed x1, local copies, waits for them, and re-layouts  1.89 us

profile of v5, /device:TPU:0, one launch (start us, length us, event | category | flops | bytes accessed | tf_op | source)
XLA Modules:
  0.0 33.7 jit_solution(7628468519897868598)
XLA Ops:
  0.0 31.9 %shard_map.91 = f32[4,4,64,128]{3,2,1,0:T(8,128)} custom-call(f32[4]{0:T(128)} %energies.1, f32[4,4,64,128]{3,2,1,0:T(8,128)} %wave_in.1, f32[4,64,128]{2,1,0:T(8,128)} %potential_in.1, s32[32,256]{1,0:T(8,128)} %index_in.1, f32[256,256]{1,0:T(8,128)} %bitcast.4, s32[1,32]{1,0:T(1,128)} %bitcast.7, s32[384]{0:T(512)} %atom_rank_in.1, f32[8,8,24]{2,1,0:T(8,128)} %bitcast.5, ...), custom_call_target="tpu_custom_call" | custom-call | tf_op jit(solution)/shard_map/pallas_call | solution.py:280
  31.9 1.9 %copy.11 = f32[4,4,64,128]{3,2,1,0:T(8,128)} copy(f32[4,4,64,128]{3,2,1,0:T(8,128)} %shard_map.91) | data formatting | bytes 1048576

commit v6 on v5

--- a/solution.py
+++ b/solution.py
@@ -55,9 +55,9 @@
 
 def kernel(
     n_dom, unroll,
-    energies, wave_in, potential_in, index_in, values_in, slot_atom_in, atom_rank_in, d_in, q_in,
+    energies, wave_in, index_in, values_in, slot_atom_in, atom_rank_in, d_in, q_in,
     out,
-    wave, potential, index, values, slot_atom, atom_rank, d_part, q_part, load_sem,
+    wave, index, values, slot_atom, atom_rank, d_part, q_part, load_sem,
     low_halo, high_halo, turned, row_hot, col_hot, picked, back_rows, acc,
     parts, arrived, windows, send_sem, recv_sem,
 ):
@@ -79,7 +79,6 @@
         for k, (src, dst) in enumerate((
             (wave_in, wave), (index_in, index), (slot_atom_in, slot_atom),
             (atom_rank_in, atom_rank), (values_in, values), (d_in, d_part), (q_in, q_part),
-            (potential_in, potential),
         ))
     ]
     for c in loads:
@@ -191,13 +190,10 @@
                 for k in (x - 2, x + 2):
                     if 0 <= k < planes:
                         far = far + wave[n, k]
-                out[n, x] = (
-                    (3.75 + potential[x] - energies[n]) * f - (2.0 / 3.0) * near + (1.0 / 24.0) * far
-                )
+                out[n, x] = 3.75 * f - (2.0 / 3.0) * near + (1.0 / 24.0) * far
 
     half = slots // unroll // 2
     lax.fori_loop(0, half, hots, 0)
-    loads[7].wait()
     local(range(bands // 2))
 
     total = parts[2]
@@ -277,22 +273,21 @@
     f32, bf16 = jnp.float32, jnp.bfloat16
     vmem = pl.BlockSpec(memory_space=pltpu.VMEM)
     atom_block = (bands * nproj, LANES)
-    return pl.pallas_call(
+    rest = pl.pallas_call(
         functools.partial(kernel, lax.axis_size("dom"), 4),
         out_shape=jax.ShapeDtypeStruct(wave.shape, f32),
         in_specs=[pl.BlockSpec(memory_space=pltpu.SMEM)]
-        + [pl.BlockSpec(memory_space=pltpu.HBM)] * 8,
+        + [pl.BlockSpec(memory_space=pltpu.HBM)] * 7,
         out_specs=vmem,
         scratch_shapes=[
             pltpu.VMEM(wave.shape, f32),
-            pltpu.VMEM(potential.shape, f32),
             pltpu.VMEM(proj_index.shape, jnp.int32),
             pltpu.VMEM((slots * nproj, pts), f32),
             pltpu.VMEM((1, slots), jnp.int32),
             pltpu.VMEM(atom_rank.shape, jnp.int32),
             pltpu.VMEM((nproj, nproj, atoms_dev), f32),
             pltpu.VMEM((nproj, nproj, atoms_dev), f32),
-            pltpu.SemaphoreType.DMA((8,)),
+            pltpu.SemaphoreType.DMA((7,)),
             pltpu.VMEM((bands, 2, ny, nz), f32),
             pltpu.VMEM((bands, 2, ny, nz), f32),
             pltpu.VMEM((2 * bands * nz, rows), bf16),
@@ -311,11 +306,12 @@
             collective_id=0, has_side_effects=True, vmem_limit_bytes=60 * 1024 * 1024
         ),
     )(
-        energies, wave, potential, proj_index,
+        energies, wave, proj_index,
         proj_values.reshape(slots * nproj, pts),
         slot_atom.reshape(1, slots), atom_rank,
         jnp.transpose(d_matrix, (1, 2, 0)), jnp.transpose(q_matrix, (1, 2, 0)),
     )
+    return rest + (potential[None] - energies[:, None, None, None]) * wave
 
 
 def solution(mesh):

time: 33.9 us -> 34.2 us (level)
  other arithmetic: 0 us -> 1.99 us
  local copies, waits for them, and re-layouts: 1.89 us -> 0.01 us
    add x0 -> x1, other arithmetic: none -> 1.99 us  [per_device(): return rest + (potential[None] - energies[:, None, None, None]) * wave]
    unnamed x1 -> x6, local copies, waits for them, and re-layouts: 1.89 us -> 0.01 us
where the time goes in v6:
time: 34.2 us; the launch traced here: 34 us
  Pallas kernels  32 us (94%)
  other arithmetic  1.99 us (6%)
    pallas_call x1, Pallas kernels, per_device(): pl.pallas_call(functools.partial(kernel, lax.axis_size('dom'), 4), out_sh...  32 us
    add x1, other arithmetic, per_device(): return rest + (potential[None] - energies[:, None, None, None]) * wave  1.99 us

profile of v6, /device:TPU:0, one launch (start us, length us, event | category | flops | bytes accessed | tf_op | source)
XLA Modules:
  0.0 34.0 jit_solution(17071617885286197654)
XLA Ops:
  0.0 0.0 copy-start
  0.0 0.0 copy-start.1
  0.0 0.0 copy-start.2
  0.0 32.0 %shard_map.91 = f32[4,4,64,128]{3,2,1,0:T(8,128)} custom-call(f32[4]{0:T(128)} %energies.1, f32[4,4,64,128]{3,2,1,0:T(8,128)} %wave_in.1, s32[32,256]{1,0:T(8,128)} %index_in.1, f32[256,256]{1,0:T(8,128)} %bitcast.4, s32[1,32]{1,0:T(1,128)} %bitcast.7, s32[384]{0:T(512)} %atom_rank_in.1, f32[8,8,24]{2,1,0:T(8,128)} %bitcast.5, f32[8,8,24]{2,1,0:T(8,128)} %bitcast.6), custom_call_target="tpu_custom_call" | custom-call | tf_op jit(solution)/shard_map/pallas_call | solution.py:276
  32.0 0.0 copy-done
  32.0 0.0 copy-done.1
  32.0 0.0 copy-done.2
  32.0 2.0 %multiply_add_fusion = f32[4,4,64,128]{3,2,1,0:T(8,128)} fusion(f32[4,4,64,128]{3,2,1,0:T(8,128)} %shard_map.91, f32[4,4,64,128]{3,2,1,0:T(8,128)S(1)} %copy-done, f32[4]{0:T(128)S(1)} %copy-done.2, f32[4,64,128]{2,1,0:T(8,128)S(1)} %copy-done.1), kind=kLoop, calls=%fused_computation | loop fusion | flops 393216 | bytes 1703952 | tf_op jit(solution)/shard_map/add | solution.py:314
Async XLA Ops:
  0.0 32.0 %copy-start = (f32[4,4,64,128]{3,2,1,0:T(8,128)S(1)}, f32[4,4,64,128]{3,2,1,0:T(8,128)}, u32[]{:S(2)}) copy-start(f32[4,4,64,128]{3,2,1,0:T(8,128)} %wave_in.1) | copy-start | bytes 1572868
  0.0 32.0 %copy-start.1 = (f32[4,64,128]{2,1,0:T(8,128)S(1)}, f32[4,64,128]{2,1,0:T(8,128)}, u32[]{:S(2)}) copy-start(f32[4,64,128]{2,1,0:T(8,128)} %param.10) | copy-start | bytes 393220
  0.0 32.0 %copy-start.2 = (f32[4]{0:T(128)S(1)}, f32[4]{0:T(128)}, u32[]{:S(2)}) copy-start(f32[4]{0:T(128)} %energies.1) | copy-start | bytes 52

commit v7 on v5

--- a/solution.py
+++ b/solution.py
@@ -278,7 +278,7 @@
     vmem = pl.BlockSpec(memory_space=pltpu.VMEM)
     atom_block = (bands * nproj, LANES)
     return pl.pallas_call(
-        functools.partial(kernel, lax.axis_size("dom"), 4),
+        functools.partial(kernel, lax.axis_size("dom"), 8),
         out_shape=jax.ShapeDtypeStruct(wave.shape, f32),
         in_specs=[pl.BlockSpec(memory_space=pltpu.SMEM)]
         + [pl.BlockSpec(memory_space=pltpu.HBM)] * 8,

time: 33.9 us -> 33 us (0.973)
  Pallas kernels: 31.9 us -> 30.9 us
    pallas_call x1, Pallas kernels: 31.9 us -> 30.9 us  [per_device(): pl.pallas_call(functools.partial(kernel, lax.axis_size('dom'), 8), out_sh...]
where the time goes in v7:
time: 33 us; the launch traced here: 32.8 us
  Pallas kernels  30.9 us (94%)
  local copies, waits for them, and re-layouts  1.89 us (6%)
    pallas_call x1, Pallas kernels, per_device(): pl.pallas_call(functools.partial(kernel, lax.axis_size('dom'), 8), out_sh...  30.9 us
    unnamed x1, local copies, waits for them, and re-layouts  1.89 us

profile of v7, /device:TPU:0, one launch (start us, length us, event | category | flops | bytes accessed | tf_op | source)
XLA Modules:
  0.0 32.8 jit_solution(7273737483140316328)
XLA Ops:
  0.0 30.9 %shard_map.91 = f32[4,4,64,128]{3,2,1,0:T(8,128)} custom-call(f32[4]{0:T(128)} %energies.1, f32[4,4,64,128]{3,2,1,0:T(8,128)} %wave_in.1, f32[4,64,128]{2,1,0:T(8,128)} %potential_in.1, s32[32,256]{1,0:T(8,128)} %index_in.1, f32[256,256]{1,0:T(8,128)} %bitcast.4, s32[1,32]{1,0:T(1,128)} %bitcast.7, s32[384]{0:T(512)} %atom_rank_in.1, f32[8,8,24]{2,1,0:T(8,128)} %bitcast.5, ...), custom_call_target="tpu_custom_call" | custom-call | tf_op jit(solution)/shard_map/pallas_call | solution.py:280
  30.9 1.9 %copy.11 = f32[4,4,64,128]{3,2,1,0:T(8,128)} copy(f32[4,4,64,128]{3,2,1,0:T(8,128)} %shard_map.91) | data formatting | bytes 1048576

commit v8 on v7

--- a/solution.py
+++ b/solution.py
@@ -278,7 +278,7 @@
     vmem = pl.BlockSpec(memory_space=pltpu.VMEM)
     atom_block = (bands * nproj, LANES)
     return pl.pallas_call(
-        functools.partial(kernel, lax.axis_size("dom"), 8),
+        functools.partial(kernel, lax.axis_size("dom"), 16),
         out_shape=jax.ShapeDtypeStruct(wave.shape, f32),
         in_specs=[pl.BlockSpec(memory_space=pltpu.SMEM)]
         + [pl.BlockSpec(memory_space=pltpu.HBM)] * 8,

time: 33 us -> 32.7 us (level)
  no operation moved by 1% of the time
where the time goes in v8:
time: 32.7 us; the launch traced here: 32.6 us
  Pallas kernels  30.7 us (94%)
  local copies, waits for them, and re-layouts  1.89 us (6%)
    pallas_call x1, Pallas kernels, per_device(): pl.pallas_call(functools.partial(kernel, lax.axis_size('dom'), 16), out_s...  30.7 us
    unnamed x1, local copies, waits for them, and re-layouts  1.89 us

profile of v8, /device:TPU:0, one launch (start us, length us, event | category | flops | bytes accessed | tf_op | source)
XLA Modules:
  0.0 32.6 jit_solution(9438661243502332778)
XLA Ops:
  0.0 30.7 %shard_map.91 = f32[4,4,64,128]{3,2,1,0:T(8,128)} custom-call(f32[4]{0:T(128)} %energies.1, f32[4,4,64,128]{3,2,1,0:T(8,128)} %wave_in.1, f32[4,64,128]{2,1,0:T(8,128)} %potential_in.1, s32[32,256]{1,0:T(8,128)} %index_in.1, f32[256,256]{1,0:T(8,128)} %bitcast.4, s32[1,32]{1,0:T(1,128)} %bitcast.7, s32[384]{0:T(512)} %atom_rank_in.1, f32[8,8,24]{2,1,0:T(8,128)} %bitcast.5, ...), custom_call_target="tpu_custom_call" | custom-call | tf_op jit(solution)/shard_map/pallas_call | solution.py:280
  30.7 1.9 %copy.11 = f32[4,4,64,128]{3,2,1,0:T(8,128)} copy(f32[4,4,64,128]{3,2,1,0:T(8,128)} %shard_map.91) | data formatting | bytes 1048576
